TPU v7x, 256 devices: a whole 4x4x8 slice. The times are simulated.
256 devices in a mesh: dp: 64 (over z, x, core), seq: 4 (over y).
Axes of the slice: x: 4, y: 4, z: 8, core: 2. Of those that a mesh axis runs over, the one named last changes fastest.
Arguments:
- hidden_in: bfloat16 [65536, 4096], P(('dp', 'seq')), may hold values from -24 to 24
- bc_weight: bfloat16 [4096, 256], P('dp'), may hold values from -0.09375 to 0.09375
- values: bfloat16 [65536, 4096], P(('dp', 'seq')), may hold values from -6 to 6
- teacher: bfloat16 [65536, 4096], P(('dp', 'seq')), may hold values from -6 to 6
- decay_codes: int32 [65536, 64], P(('dp', 'seq')), may hold values from 0 to 15
- resets: int32 [65536], P(('dp', 'seq')), may hold values 0 or 1
- head_decay_rates: float32 [64], replicated, may hold values from 0.25 to 100
- skip_gain: float32 [64], replicated, may hold values from 0.5 to 1.5
- confidence: int32 [65536], P(('dp', 'seq')), may hold values from 1 to 8
Outputs:
- values_grad: bfloat16 [65536, 4096], P(('dp', 'seq'))
- hidden_grad: bfloat16 [65536, 4096], P(('dp', 'seq'))
- weight_grad: float32 [4096, 256], P('dp')
All inputs are finite; a program needn't handle non-finite values. No bound on the sum of `resets` on one device may be relied on, other than what follows from the above.
Results may differ from a plain program's by a relative error of at most 0.011.
Values may be sent and summed in bfloat16 or wider, within the bound.
No kernel may reach another device: no remote copies, remote signals or barrier semaphores. Data moves between devices by JAX's collectives and lax.ppermute only.
A program may use at most 128 MiB of HBM per device.

v0:
```python
import math
import jax
import jax.numpy as jnp
from jax import lax
from jax.sharding import PartitionSpec as P

GROUP = 256
SPIKE_MULTIPLIER = 3000.0
STEP_FACTOR = 16.0


def carried_in(x, axis, combine, identity):
    peers, place = (lax.axis_size(axis), lax.axis_index(axis))
    everything = jax.tree.map(lambda part: lax.all_gather(part, axis), x)
    start = jax.tree.map(
        lambda part, zero: jnp.broadcast_to(jnp.asarray(zero, part.dtype), part.shape), x, identity
    )

    def carried_step(k, before):
        reached = k < place
        new = combine(before, jax.tree.map(lambda part: part[k], everything))
        return jax.tree.map(lambda a, b: jnp.where(reached, a, b), new, before)

    return lax.fori_loop(0, peers, carried_step, start)


def prefix(x, axis, combine, identity):
    peers, place = (lax.axis_size(axis), lax.axis_index(axis))
    everything = jax.tree.map(
        lambda part, kind: lax.all_gather(part.astype(kind), axis), x, (jnp.bfloat16, jnp.bfloat16)
    )
    start = jax.tree.map(
        lambda part, zero: jnp.broadcast_to(jnp.asarray(zero, part.dtype), part.shape), x, identity
    )

    def prefix_step(k, before):
        at = peers - 1 - k
        reached = at > place
        new = combine(
            before, jax.tree.map(lambda part, own: part[at].astype(own.dtype), everything, x)
        )
        return jax.tree.map(lambda a, b: jnp.where(reached, a, b), new, before)

    return lax.fori_loop(0, peers, prefix_step, start)


def decay_terms(decay_codes, resets, head_decay_rates):
    logarithm_floor = jnp.log(0.9995 + 0.0004 * decay_codes.astype(jnp.float32) / 15.0)
    decay_logarithm = (
        head_decay_rates[None, :]
        * (1.0 + SPIKE_MULTIPLIER * resets.astype(jnp.float32))[:, None]
        * logarithm_floor
    )
    return (decay_logarithm, -STEP_FACTOR * logarithm_floor)


def combine(earlier, later):
    return (earlier[0] + later[0], jnp.exp(later[0])[:, None, None] * earlier[1] + later[1])


def body(
    hidden_in,
    bc_weight,
    values,
    teacher,
    decay_codes,
    resets,
    head_decay_rates,
    skip_gain,
    confidence,
):
    length = hidden_in.shape[0]
    blocks = length // GROUP
    head_count = decay_codes.shape[1]
    head_size = values.shape[1] // head_count
    state_size = bc_weight.shape[1] // 2
    seq_count = lax.axis_size("seq")
    doc_len = length * seq_count
    all_tokens = doc_len * lax.axis_size("dp")
    conf_float = confidence.astype(jnp.float32)
    conf_total = lax.psum(jnp.sum(conf_float), "seq")
    full_weight = lax.all_gather(bc_weight, "dp", axis=0, tiled=True)
    bc_acc = jnp.dot(hidden_in, full_weight, preferred_element_type=jnp.float32)
    bc_rows = bc_acc.astype(jnp.bfloat16).reshape(blocks, GROUP, 2 * state_size)
    input_map = bc_rows[:, :, :state_size]
    output_map = bc_rows[:, :, state_size:]
    decay_logarithm, step_size = decay_terms(decay_codes, resets, head_decay_rates)
    cumulative = jnp.cumsum(decay_logarithm.reshape(blocks, GROUP, head_count), axis=1)
    step_blk = step_size.reshape(blocks, GROUP, head_count)
    block_log = cumulative[:, -1, :]
    tail_decay = jnp.exp(block_log[:, None, :] - cumulative)
    leading_decay = jnp.exp(cumulative)
    cum_heads = jnp.transpose(cumulative, (0, 2, 1))
    lower_tri = lax.broadcasted_iota(jnp.int32, (GROUP, GROUP), 0) >= lax.broadcasted_iota(
        jnp.int32, (GROUP, GROUP), 1
    )
    spread = jnp.where(lower_tri, cum_heads[:, :, :, None] - cum_heads[:, :, None, :], 0.0)
    decay_grid = (
        jnp.where(lower_tri, jnp.exp(spread), 0.0)
        * jnp.transpose(step_blk, (0, 2, 1))[:, :, None, :]
    )
    intersection = jnp.einsum(
        "btn,bsn->bts", output_map, input_map, preferred_element_type=jnp.float32
    )
    mixing = (intersection[:, None] * decay_grid).astype(jnp.bfloat16)
    value_blocks = values.reshape(blocks, GROUP, head_count, head_size)
    write_scale = tail_decay * step_blk
    value_scaled = (write_scale[..., None] * value_blocks).astype(jnp.bfloat16)
    local_state = jnp.einsum(
        "bshp,bsn->bhpn", value_scaled, input_map, preferred_element_type=jnp.float32
    )
    zero_state = jnp.zeros((head_count, head_size, state_size), jnp.float32)
    zero_log = jnp.zeros((head_count,), jnp.float32)
    running_state = zero_state
    running_log = zero_log
    position = 0
    prefix_states = running_state
    prefix_logs = running_log
    running_state = (
        jnp.exp(block_log[position])[:, None, None] * running_state + local_state[position]
    )
    running_log = block_log[position]
    device_log = running_log
    entry_device = carried_in((device_log, running_state), "seq", combine, (zero_log, zero_state))[
        1
    ]
    entry_state = jnp.stack([jnp.exp(prefix_logs)[:, None, None] * entry_device + prefix_states])
    entry_bf = entry_state.astype(jnp.bfloat16)
    outputs = jnp.einsum(
        "bhts,bshp->bthp", mixing, value_blocks, preferred_element_type=jnp.float32
    )
    outputs = outputs + leading_decay[..., None] * jnp.einsum(
        "btn,bhpn->bthp", output_map, entry_bf, preferred_element_type=jnp.float32
    )
    outputs = outputs + skip_gain[None, None, :, None] * value_blocks
    token_weight = conf_float * doc_len / conf_total
    target = teacher.reshape(blocks, GROUP, head_count, head_size)
    out_grad = (token_weight.reshape(blocks, GROUP)[:, :, None, None] * (outputs - target)).astype(
        jnp.bfloat16
    )
    out_scaled = (leading_decay[..., None] * out_grad).astype(jnp.bfloat16)
    state_pull = jnp.einsum(
        "bthp,btn->bhpn", out_scaled, output_map, preferred_element_type=jnp.float32
    )
    suffix_grads = [zero_state] * blocks
    suffix_logs = [zero_log] * blocks
    running_grad = zero_state
    running_log = zero_log
    position = 0
    suffix_grads[position] = running_grad
    suffix_logs[position] = running_log
    running_grad = jnp.exp(block_log[position])[:, None, None] * running_grad + state_pull[position]
    after_grad = prefix((device_log, running_grad), "seq", combine, (zero_log, zero_state))[1]
    exit_grad = jnp.stack([jnp.exp(suffix_logs[0])[:, None, None] * after_grad + suffix_grads[0]])
    exit_bf = exit_grad.astype(jnp.bfloat16)
    pair_dots = jnp.einsum(
        "bthp,bshp->bhts", out_grad, value_blocks, preferred_element_type=jnp.float32
    )
    score_grad = jnp.sum(pair_dots * decay_grid, axis=1).astype(jnp.bfloat16)
    values_grad = jnp.einsum(
        "bhts,bthp->bshp", mixing, out_grad, preferred_element_type=jnp.float32
    )
    values_grad = values_grad + write_scale[..., None] * jnp.einsum(
        "bsn,bhpn->bshp", input_map, exit_bf, preferred_element_type=jnp.float32
    )
    values_grad = values_grad + skip_gain[None, None, :, None] * out_grad
    input_grad = jnp.einsum(
        "bts,btn->bsn", score_grad, output_map, preferred_element_type=jnp.float32
    )
    input_grad = input_grad + jnp.einsum(
        "bshp,bhpn->bsn", value_scaled, exit_bf, preferred_element_type=jnp.float32
    )
    output_grad = jnp.einsum(
        "bts,bsn->btn", score_grad, input_map, preferred_element_type=jnp.float32
    )
    output_grad = output_grad + jnp.einsum(
        "bthp,bhpn->btn", out_scaled, entry_bf, preferred_element_type=jnp.float32
    )
    bc_grad = (
        jnp.concatenate([input_grad, output_grad], axis=2)
        .reshape(length, 2 * state_size)
        .astype(jnp.bfloat16)
    )
    contract_cols = (((1,), (1,)), ((), ()))
    hidden_acc = lax.dot_general(
        bc_grad, full_weight, contract_cols, preferred_element_type=jnp.float32
    )
    hidden_grad = hidden_acc.astype(jnp.bfloat16)
    contract_rows = (((0,), (0,)), ((), ()))
    local_rows = bc_weight.shape[0]
    full_term = lax.dot_general(
        hidden_in, bc_grad, contract_rows, preferred_element_type=jnp.float32
    )
    summed = lax.psum(full_term, ("dp", "seq"))
    own_rows = lax.dynamic_slice_in_dim(summed, lax.axis_index("dp") * local_rows, local_rows, 0)
    weight_grad = own_rows / math.sqrt(all_tokens)
    return (
        values_grad.reshape(length, head_count * head_size).astype(jnp.bfloat16),
        hidden_grad,
        weight_grad,
    )


def solution(mesh):
    return jax.shard_map(
        body,
        mesh=mesh,
        in_specs=(
            P(("dp", "seq"), None),
            P("dp", None),
            P(("dp", "seq"), None),
            P(("dp", "seq"), None),
            P(("dp", "seq"), None),
            P(("dp", "seq")),
            P(),
            P(),
            P(("dp", "seq")),
        ),
        out_specs=(P(("dp", "seq"), None), P(("dp", "seq"), None), P("dp", None)),
        check_vma=False,
    )
```

profile of v0, /device:TPU:2, one launch (start us, length us, event | category | flops | bytes accessed | tf_op | source)
XLA Modules:
  0.0 555.4 jit_solution(11231758227764263669)
XLA Ops:
  7.2 0.0 all-gather.8.cloned.1.call-start
  7.2 0.7 all-gather.8.cloned.1.call-update
  7.9 0.0 all-gather.10.cloned.1.call-start
  8.0 0.9 copy.61
  8.9 0.7 multiply_add_fusion
  9.6 0.8 multiply_bitcast_fusion
  10.3 0.1 copy.62
  10.4 0.6 reduce-window.6
  11.0 0.1 copy.67
  11.1 0.2 slice_reduce_fusion
  11.3 0.1 copy.68
  11.5 0.1 fusion.35
  11.5 0.1 copy.70
  11.6 4.1 copy.66
  15.7 3.3 fusion.11
  19.0 71.0 %all-gather.8.cloned.1.call-done = bf16[4096,256]{1,0:T(8,128)(2,1)} async-done(((bf16[64,256]{1,0:T(8,128)(2,1)}), bf16[4096,256]{1,0:T(8,128)(2,1)}) %all-gather.8.cloned.1.call-update) | async-done | bytes 2097168 | tf_op jit(solution)/shard_map/all_gather | solution.py:82
  90.1 2.4 fusion.24
  92.5 2.1 convolution_add_fusion
  94.6 0.0 all-gather.12.cloned.1.call-start
  94.7 0.6 copy-done.8
  95.3 0.6 convert_reduce_fusion
  95.9 11.1 %psum.14 = f32[]{:T(128)} all-reduce(f32[]{:T(128)} %convert_reduce_fusion), channel_id=1, replica_groups=mesh['dp'=64,'seq'=4] {'seq'}, use_global_device_ids=true, to_apply=%region_1.0 | all-reduce | flops 1 | bytes 8 | tf_op jit(solution)/shard_map/psum | solution.py:81
  107.0 0.1 copy.63
  107.1 0.1 copy.69
  107.2 0.1 copy.76
  107.2 0.1 copy.65
  107.3 4.4 copy.72
  111.8 6.9 %all-gather = f32[4,1,64]{2,1,0:T(1,128)S(1)} all-gather(f32[1,1,64]{2,1,0:T(1,128)S(1)} %get-tuple-element.317), channel_id=2, replica_groups=mesh['dp'=64,'seq'=4] {'seq'}, dimensions={0}, use_global_device_ids=true | all-gather | bytes 1280 | tf_op jit(solution)/shard_map/all_gather | solution.py:14
  118.7 0.7 multiply_divide_fusion
  119.4 0.2 fusion.41
  119.6 59.5 %all-gather.10.cloned.1.call-done = f32[256,64,128]{2,1,0:T(8,128)} async-done(((f32[64,64,128]{2,1,0:T(8,128)}), f32[256,64,128]{2,1,0:T(8,128)}) %all-gather.10.cloned.1.call-update) | async-done | bytes 8388624 | tf_op jit(solution)/shard_map/all_gather | solution.py:14
  179.1 14.9 %while.30 = (s32[]{:T(128)}, f32[64,64,128]{2,1,0:T(8,128)}, s32[]{:T(128)}, f32[4,64]{1,0:T(4,128)S(1)}, f32[4,64,64,128]{3,2,1,0:T(8,128)}, /*index=5*/s32[]{:T(128)}, s32[]{:T(128)}) while((s32[]{:T(128)}, f32[64,64,128]{2,1,0:T(8,128)}, s32[]{:T(128)}, f32[4,64]{1,0:T(4,128)S(1)}, f32[4,64,64,128]{3,2,1,0:T(8,128)}, ...), condition=%wide.region_5.6_spmd.clone, body=%wide.region_4.5_spmd.clone.sunk | while | flops 2097156 | bytes 6292329 | solution.py:24
  179.1 3.2 fusion.71
  182.4 3.9 fusion.71
  186.3 3.9 fusion.71
  190.2 3.9 fusion.71
  194.0 2.4 fusion.33
  196.5 1.0 copy-done.4
  197.5 6.2 %fusion.10 = bf16[1,256,64,64]{1,3,2,0:T(8,128)(2,1)S(1)} fusion(f32[1,256,64,64]{1,3,2,0:T(8,128)S(1)} %bitcast.161, f32[256,64,64]{0,2,1:T(8,128)S(1)} %fusion.33, bf16[256,64,64]{0,2,1:T(8,128)(2,1)S(1)} %bitcast.157, f32[64,256]{1,0:T(8,128)S(1)} %copy.65, f32[64,256]{1,0:T(8,128)S(1)} %bitcast_add_fusion.4, f32[256,256]{1,0:T(8,128)S(1)} %fusion.41, ...), kind=kOutput, calls=%fused_computation.23 | convolution fusion | flops 570425344 | bytes 15205632 | tf_op jit(solution)/shard_map/bhts,bshp->bthp/dot_general | solution.py:129
  203.7 1.3 copy-done.5
  205.0 1.7 add_convert_fusion
  206.7 0.0 all-gather.12.cloned.1.call-update
  206.7 0.0 all-reduce.2.cloned.1.call-start
  206.8 8.8 %all-gather.3 = bf16[4,1,64]{2,1,0:T(2,128)(2,1)S(1)} all-gather(bf16[1,1,64]{2,1,0:T(2,128)(2,1)S(1)} %slice.61), channel_id=5, replica_groups=mesh['dp'=64,'seq'=4] {'seq'}, dimensions={0}, use_global_device_ids=true | all-gather | bytes 640 | tf_op jit(solution)/shard_map/all_gather | solution.py:30
  215.6 3.0 fusion.21
  218.6 0.5 copy-done.6
  219.1 6.9 %multiply_reduce_fusion = bf16[256,256]{1,0:T(8,128)(2,1)S(1)} fusion(bf16[256,64,64]{0,2,1:T(8,128)(2,1)S(1)} %bitcast.159, f32[64,256]{1,0:T(8,128)S(1)} %copy.65, f32[64,256]{1,0:T(8,128)S(1)} %bitcast_add_fusion.4, pred[256,256]{1,0:T(8,128)(4,1)S(1)} %iota_compare_fusion, bf16[1,256,64,64]{1,3,2,0:T(8,128)(2,1)S(1)} %copy-done.6), kind=kOutput, calls=%fused_computation.6 | convolution fusion | flops 561971200 | bytes 4521984 | tf_op jit(solution)/shard_map/bthp,bshp->bhts/dot_general | solution.py:156
  226.0 0.2 fusion.27
  226.3 32.4 %all-gather.12.cloned.1.call-done = bf16[256,64,128]{2,1,0:T(8,128)(2,1)} async-done(((bf16[64,64,128]{2,1,0:T(8,128)(2,1)}), bf16[256,64,128]{2,1,0:T(8,128)(2,1)}) %all-gather.12.cloned.1.call-update) | async-done | bytes 4194320 | tf_op jit(solution)/shard_map/all_gather | solution.py:30
  258.7 13.7 %while.31 = (s32[]{:T(128)}, f32[64,64,128]{2,1,0:T(8,128)}, s32[]{:T(128)}, bf16[4,64]{1,0:T(4,128)(2,1)S(1)}, bf16[4,64,64,128]{3,2,1,0:T(8,128)(2,1)}, /*index=5*/s32[]{:T(128)}, s32[]{:T(128)}, s32[]{:T(128)}, s32[]{:T(128)}) while((s32[]{:T(128)}, f32[64,64,128]{2,1,0:T(8,128)}, s32[]{:T(128)}, bf16[4,64]{1,0:T(4,128)(2,1)S(1)}, ...), condition=%wide.region_7.8_spmd.clone, body=%wide.region_6.7_spmd.clone.sunk | while | flops 2621512 | bytes 5243687 | solution.py:44
  258.7 3.0 fusion.72
  261.7 3.6 fusion.72
  265.2 3.6 fusion.72
  268.8 3.6 fusion.72
  272.4 2.8 convolution_bitcast_fusion.1
  275.2 0.2 fusion.28
  275.4 2.7 convolution_bitcast_fusion
  278.1 2.4 fusion.30
  280.6 6.8 %fusion.6 = bf16[1,256,64,64]{1,3,2,0:T(8,128)(2,1)} fusion(bf16[1,256,64,64]{1,3,2,0:T(8,128)(2,1)S(1)} %copy-done.7, f32[256,64,64]{0,2,1:T(8,128)S(1)} %fusion.30, f32[64,256]{1,0:T(8,128)S(1)} %copy.65, f32[64,256]{1,0:T(8,128)S(1)} %bitcast_add_fusion.4, f32[256,256]{1,0:T(8,128)S(1)} %fusion.41, pred[256,256]{1,0:T(8,128)(4,1)S(1)} %iota_compare_fusion, ...), kind=kOutput, calls=%fused_computation.17 | convolution fusion | flops 568328192 | bytes 8913152 | tf_op jit(solution)/shard_map/bhts,bthp->bshp/dot_general | solution.py:160
  287.4 4.1 copy.74
  291.5 3.7 convolution_convert_fusion
  295.2 252.0 %all-reduce.2.cloned.1.call-done = f32[4096,256]{0,1:T(8,128)} async-done(((f32[4096,256]{0,1:T(8,128)}), f32[4096,256]{0,1:T(8,128)}) %all-reduce.2.cloned.1.call-update) | async-done | bytes 4194320 | tf_op jit(solution)/shard_map/psum | solution.py:194
  547.2 1.0 dynamic-slice_multiply_fusion
  548.2 0.7 copy.75
  (38 shorter events, 0.3 us)
Async XLA Ops:
  7.2 82.9 %copy-start = (bf16[256,4096]{1,0:T(8,128)(2,1)S(1)}, bf16[256,4096]{1,0:T(8,128)(2,1)}, u32[]{:S(2)}) copy-start(bf16[256,4096]{1,0:T(8,128)(2,1)} %param.13) | copy-start | bytes 6291460
  7.2 82.9 %all-gather.8.cloned.1.call-start = ((), (), s32[]{:S(2)}) async-start(), calls=%async_computation | async-start | bytes 2129920 | tf_op jit(solution)/shard_map/all_gather | solution.py:82
  7.9 171.2 %all-gather.10.cloned.1.call-start = ((), (), s32[]{:S(2)}) async-start(), calls=%async_computation.2 | async-start | bytes 10485760 | tf_op jit(solution)/shard_map/all_gather | solution.py:14
  90.1 2.5 copy-start.1
  94.6 0.7 copy-start.8
  94.6 164.1 %all-gather.12.cloned.1.call-start = ((), (), s32[]{:S(2)}) async-start(), calls=%async_computation.3 | async-start | bytes 5242880 | tf_op jit(solution)/shard_map/all_gather | solution.py:30
  194.0 2.5 copy-start.2
  194.0 3.5 copy-start.4
  194.0 3.5 copy-start.9
  203.7 1.4 copy-start.5
  206.7 340.5 %all-reduce.2.cloned.1.call-start = ((), (), s32[]{:S(2)}) async-start(), calls=%async_computation.1 | async-start | bytes 8388608 | tf_op jit(solution)/shard_map/psum | solution.py:194
  215.6 3.0 copy-start.3
  215.6 3.5 copy-start.6
  278.1 2.5 copy-start.7
Sparse Core Ops, SparseCore 0:
  10.8 79.2 all-gather.7
  94.7 84.3 all-gather.9
  206.9 51.7 all-gather.11
  278.2 268.8 all-reduce.1
where the time goes:
time: 556 us; the launch traced here: 555 us
  waiting for transfers between devices  416 us (75%)
  matrix products  43.8 us (8%)
  other arithmetic  36.4 us (7%)
  blocking collectives  26.8 us (5%)
  local copies, waits for them, and re-layouts  18.5 us (3%)
  between operations  14 us (3%)
    psum x1, waiting for transfers between devices, body(): summed = lax.psum(full_term, ('dp', 'seq'))  252 us
    all_gather x1, waiting for transfers between devices, body(): full_weight = lax.all_gather(bc_weight, 'dp', axis=0, tiled=True)  71 us
    all_gather x1, waiting for transfers between devices, carried_in(): everything = jax.tree.map(lambda part: lax.all_gather(part, axis), x)  59.5 us
    all_gather x1, waiting for transfers between devices, prefix(): lax.all_gather(part.astype(kind), axis)  32.4 us
    select_n x4, other arithmetic, carried_step(): return jax.tree.map(lambda a, b: jnp.where(reached, a, b), new, before)  14.9 us
    select_n x4, other arithmetic, prefix_step(): return jax.tree.map(lambda a, b: jnp.where(reached, a, b), new, before)  13.7 us
    unnamed x25, local copies, waits for them, and re-layouts  13.3 us
    psum x1, blocking collectives, body(): conf_total = lax.psum(jnp.sum(conf_float), 'seq')  11.1 us
  transfers between devices with their start and end apart: 4, of which 4 were waited for; matrix products, arithmetic and copies ran while one was open for 8% of the time, Pallas kernels for 0%

commit v1 on v0

--- a/solution.py
+++ b/solution.py
@@ -191,7 +191,8 @@
     full_term = lax.dot_general(
         hidden_in, bc_grad, contract_rows, preferred_element_type=jnp.float32
     )
-    summed = lax.psum(full_term, ("dp", "seq"))
+    one_axis = lax.psum(full_term, "seq")
+    summed = lax.psum(one_axis, "dp")
     own_rows = lax.dynamic_slice_in_dim(summed, lax.axis_index("dp") * local_rows, local_rows, 0)
     weight_grad = own_rows / math.sqrt(all_tokens)
     return (

time: 556 us -> 585 us (1.052)
  waiting for transfers between devices: 416 us -> 444 us
    psum x1 -> x2, waiting for transfers between devices: 252 us -> 280 us  [the longest x1 182 us: body(): summed = lax.psum(one_axis, 'dp')]
  transfers between devices with their start and end apart: 4 -> 5, of which waited for: 4 -> 5; matrix products, arithmetic and copies ran while one was open for 8% -> 8% of each run, Pallas kernels for 0% -> 0%
where the time goes in v1:
time: 585 us; the launch traced here: 584 us
  waiting for transfers between devices  444 us (76%)
  matrix products  44 us (8%)
  other arithmetic  36.4 us (6%)
  blocking collectives  26.7 us (5%)
  local copies, waits for them, and re-layouts  18.5 us (3%)
  between operations  14.1 us (2%)
    psum x1, waiting for transfers between devices, body(): summed = lax.psum(one_axis, 'dp')  182 us
    psum x1, waiting for transfers between devices, body(): one_axis = lax.psum(full_term, 'seq')  98.2 us
    all_gather x1, waiting for transfers between devices, body(): full_weight = lax.all_gather(bc_weight, 'dp', axis=0, tiled=True)  71 us
    all_gather x1, waiting for transfers between devices, carried_in(): everything = jax.tree.map(lambda part: lax.all_gather(part, axis), x)  59.5 us
    all_gather x1, waiting for transfers between devices, prefix(): lax.all_gather(part.astype(kind), axis)  32.6 us
    select_n x4, other arithmetic, carried_step(): return jax.tree.map(lambda a, b: jnp.where(reached, a, b), new, before)  14.9 us
    select_n x4, other arithmetic, prefix_step(): return jax.tree.map(lambda a, b: jnp.where(reached, a, b), new, before)  13.7 us
    unnamed x25, local copies, waits for them, and re-layouts  13.2 us
  transfers between devices with their start and end apart: 5, of which 5 were waited for; matrix products, arithmetic and copies ran while one was open for 8% of the time, Pallas kernels for 0%

profile of v1, /device:TPU:2, one launch (start us, length us, event | category | flops | bytes accessed | tf_op | source)
XLA Modules:
  0.0 584.1 jit_solution(787419911868357663)
XLA Ops:
  7.2 0.7 all-gather.8.cloned.1.call-update
  7.9 0.0 all-gather.10.cloned.1.call-start
  8.0 0.9 copy.61
  8.9 0.7 multiply_add_fusion
  9.6 0.8 multiply_bitcast_fusion
  10.3 0.1 copy.62
  10.4 0.6 reduce-window.6
  11.0 0.1 copy.67
  11.1 0.2 slice_reduce_fusion
  11.3 0.1 copy.68
  11.5 0.1 fusion.35
  11.5 0.1 copy.70
  11.6 4.1 copy.66
  15.7 3.3 fusion.11
  19.0 71.0 %all-gather.8.cloned.1.call-done = bf16[4096,256]{1,0:T(8,128)(2,1)} async-done(((bf16[64,256]{1,0:T(8,128)(2,1)}), bf16[4096,256]{1,0:T(8,128)(2,1)}) %all-gather.8.cloned.1.call-update) | async-done | bytes 2097168 | tf_op jit(solution)/shard_map/all_gather | solution.py:82
  90.1 2.4 fusion.24
  92.5 2.1 convolution_add_fusion
  94.6 0.0 all-gather.12.cloned.1.call-start
  94.7 0.6 copy-done.8
  95.3 0.6 convert_reduce_fusion
  95.9 11.1 %psum.21 = f32[]{:T(128)} all-reduce(f32[]{:T(128)} %convert_reduce_fusion), channel_id=1, replica_groups=mesh['dp'=64,'seq'=4] {'seq'}, use_global_device_ids=true, to_apply=%region_1.0 | all-reduce | flops 1 | bytes 8 | tf_op jit(solution)/shard_map/psum | solution.py:81
  107.0 0.1 copy.63
  107.1 0.1 copy.69
  107.2 0.1 copy.76
  107.2 0.1 copy.65
  107.3 4.4 copy.72
  111.8 6.9 %all-gather = f32[4,1,64]{2,1,0:T(1,128)S(1)} all-gather(f32[1,1,64]{2,1,0:T(1,128)S(1)} %get-tuple-element.317), channel_id=2, replica_groups=mesh['dp'=64,'seq'=4] {'seq'}, dimensions={0}, use_global_device_ids=true | all-gather | bytes 1280 | tf_op jit(solution)/shard_map/all_gather | solution.py:14
  118.7 0.7 multiply_divide_fusion
  119.4 0.2 fusion.41
  119.6 59.5 %all-gather.10.cloned.1.call-done = f32[256,64,128]{2,1,0:T(8,128)} async-done(((f32[64,64,128]{2,1,0:T(8,128)}), f32[256,64,128]{2,1,0:T(8,128)}) %all-gather.10.cloned.1.call-update) | async-done | bytes 8388624 | tf_op jit(solution)/shard_map/all_gather | solution.py:14
  179.1 14.9 %while.30 = (s32[]{:T(128)}, f32[64,64,128]{2,1,0:T(8,128)}, s32[]{:T(128)}, f32[4,64]{1,0:T(4,128)S(1)}, f32[4,64,64,128]{3,2,1,0:T(8,128)}, /*index=5*/s32[]{:T(128)}, s32[]{:T(128)}) while((s32[]{:T(128)}, f32[64,64,128]{2,1,0:T(8,128)}, s32[]{:T(128)}, f32[4,64]{1,0:T(4,128)S(1)}, f32[4,64,64,128]{3,2,1,0:T(8,128)}, ...), condition=%wide.region_5.6_spmd.clone, body=%wide.region_4.5_spmd.clone.sunk | while | flops 2097156 | bytes 6292329 | solution.py:24
  179.1 3.2 fusion.71
  182.4 3.9 fusion.71
  186.3 3.9 fusion.71
  190.2 3.9 fusion.71
  194.0 2.4 fusion.33
  196.5 1.0 copy-done.4
  197.5 6.2 %fusion.10 = bf16[1,256,64,64]{1,3,2,0:T(8,128)(2,1)S(1)} fusion(f32[1,256,64,64]{1,3,2,0:T(8,128)S(1)} %bitcast.161, f32[256,64,64]{0,2,1:T(8,128)S(1)} %fusion.33, bf16[256,64,64]{0,2,1:T(8,128)(2,1)S(1)} %bitcast.157, f32[64,256]{1,0:T(8,128)S(1)} %copy.65, f32[64,256]{1,0:T(8,128)S(1)} %bitcast_add_fusion.4, f32[256,256]{1,0:T(8,128)S(1)} %fusion.41, ...), kind=kOutput, calls=%fused_computation.23 | convolution fusion | flops 570425344 | bytes 15205632 | tf_op jit(solution)/shard_map/bhts,bshp->bthp/dot_general | solution.py:129
  203.7 1.3 copy-done.5
  205.0 1.7 add_convert_fusion
  206.7 0.0 all-reduce.3.cloned.1.call-start
  206.8 8.6 %all-gather.3 = bf16[4,1,64]{2,1,0:T(2,128)(2,1)S(1)} all-gather(bf16[1,1,64]{2,1,0:T(2,128)(2,1)S(1)} %slice.61), channel_id=5, replica_groups=mesh['dp'=64,'seq'=4] {'seq'}, dimensions={0}, use_global_device_ids=true | all-gather | bytes 640 | tf_op jit(solution)/shard_map/all_gather | solution.py:30
  215.4 3.0 fusion.21
  218.4 0.5 copy-done.6
  218.9 6.9 %multiply_reduce_fusion = bf16[256,256]{1,0:T(8,128)(2,1)S(1)} fusion(bf16[256,64,64]{0,2,1:T(8,128)(2,1)S(1)} %bitcast.159, f32[64,256]{1,0:T(8,128)S(1)} %copy.65, f32[64,256]{1,0:T(8,128)S(1)} %bitcast_add_fusion.4, pred[256,256]{1,0:T(8,128)(4,1)S(1)} %iota_compare_fusion, bf16[1,256,64,64]{1,3,2,0:T(8,128)(2,1)S(1)} %copy-done.6), kind=kOutput, calls=%fused_computation.6 | convolution fusion | flops 561971200 | bytes 4521984 | tf_op jit(solution)/shard_map/bthp,bshp->bhts/dot_general | solution.py:156
  225.8 0.2 fusion.27
  226.0 32.6 %all-gather.12.cloned.1.call-done = bf16[256,64,128]{2,1,0:T(8,128)(2,1)} async-done(((bf16[64,64,128]{2,1,0:T(8,128)(2,1)}), bf16[256,64,128]{2,1,0:T(8,128)(2,1)}) %all-gather.12.cloned.1.call-update) | async-done | bytes 4194320 | tf_op jit(solution)/shard_map/all_gather | solution.py:30
  258.7 13.7 %while.31 = (s32[]{:T(128)}, f32[64,64,128]{2,1,0:T(8,128)}, s32[]{:T(128)}, bf16[4,64]{1,0:T(4,128)(2,1)S(1)}, bf16[4,64,64,128]{3,2,1,0:T(8,128)(2,1)}, /*index=5*/s32[]{:T(128)}, s32[]{:T(128)}, s32[]{:T(128)}, s32[]{:T(128)}) while((s32[]{:T(128)}, f32[64,64,128]{2,1,0:T(8,128)}, s32[]{:T(128)}, bf16[4,64]{1,0:T(4,128)(2,1)S(1)}, ...), condition=%wide.region_7.8_spmd.clone, body=%wide.region_6.7_spmd.clone.sunk | while | flops 2621512 | bytes 5243687 | solution.py:44
  258.7 3.0 fusion.72
  261.7 3.6 fusion.72
  265.2 3.6 fusion.72
  268.8 3.6 fusion.72
  272.4 2.8 convolution_bitcast_fusion.1
  275.2 0.2 fusion.28
  275.4 2.7 convolution_bitcast_fusion
  278.1 0.2 all-reduce.5.cloned.1.call-start
  278.4 98.2 %all-reduce.3.cloned.1.call-done = f32[4096,256]{0,1:T(8,128)} async-done(((f32[4096,256]{0,1:T(8,128)}), f32[4096,256]{0,1:T(8,128)}) %all-reduce.3.cloned.1.call-update) | async-done | bytes 4194320 | tf_op jit(solution)/shard_map/psum | solution.py:194
  376.6 2.4 fusion.30
  379.1 6.8 %fusion.6 = bf16[1,256,64,64]{1,3,2,0:T(8,128)(2,1)} fusion(bf16[1,256,64,64]{1,3,2,0:T(8,128)(2,1)S(1)} %copy-done.7, f32[256,64,64]{0,2,1:T(8,128)S(1)} %fusion.30, f32[64,256]{1,0:T(8,128)S(1)} %copy.65, f32[64,256]{1,0:T(8,128)S(1)} %bitcast_add_fusion.4, f32[256,256]{1,0:T(8,128)S(1)} %fusion.41, pred[256,256]{1,0:T(8,128)(4,1)S(1)} %iota_compare_fusion, ...), kind=kOutput, calls=%fused_computation.17 | convolution fusion | flops 568328192 | bytes 8913152 | tf_op jit(solution)/shard_map/bhts,bthp->bshp/dot_general | solution.py:160
  385.9 4.1 copy.74
  390.0 3.9 convolution_convert_fusion
  393.9 181.9 %all-reduce.5.cloned.1.call-done = f32[4096,256]{0,1:T(8,128)} async-done(((f32[4096,256]{0,1:T(8,128)}), f32[4096,256]{0,1:T(8,128)}) %all-reduce.5.cloned.1.call-update) | async-done | bytes 4194320 | tf_op jit(solution)/shard_map/psum | solution.py:195
  575.8 1.0 dynamic-slice_multiply_fusion
  576.8 0.7 copy.75
  (41 shorter events, 0.3 us)
Async XLA Ops:
  7.2 82.9 %copy-start = (bf16[256,4096]{1,0:T(8,128)(2,1)S(1)}, bf16[256,4096]{1,0:T(8,128)(2,1)}, u32[]{:S(2)}) copy-start(bf16[256,4096]{1,0:T(8,128)(2,1)} %param.13) | copy-start | bytes 6291460
  7.2 82.9 %all-gather.8.cloned.1.call-start = ((), (), s32[]{:S(2)}) async-start(), calls=%async_computation | async-start | bytes 2129920 | tf_op jit(solution)/shard_map/all_gather | solution.py:82
  7.9 171.2 %all-gather.10.cloned.1.call-start = ((), (), s32[]{:S(2)}) async-start(), calls=%async_computation.3 | async-start | bytes 10485760 | tf_op jit(solution)/shard_map/all_gather | solution.py:14
  90.1 2.5 copy-start.1
  94.6 0.7 copy-start.8
  94.6 164.1 %all-gather.12.cloned.1.call-start = ((), (), s32[]{:S(2)}) async-start(), calls=%async_computation.4 | async-start | bytes 5242880 | tf_op jit(solution)/shard_map/all_gather | solution.py:30
  194.0 2.5 copy-start.2
  194.0 3.5 copy-start.4
  194.0 3.5 copy-start.9
  203.7 1.4 copy-start.5
  206.7 169.9 %all-reduce.3.cloned.1.call-start = ((), (), s32[]{:S(2)}) async-start(), calls=%async_computation.1 | async-start | bytes 8388608 | tf_op jit(solution)/shard_map/psum | solution.py:194
  215.4 3.0 copy-start.3
  215.4 3.5 copy-start.6
  278.1 297.7 %all-reduce.5.cloned.1.call-start = ((), (), s32[]{:S(2)}) async-start(), calls=%async_computation.2 | async-start | bytes 8388608 | tf_op jit(solution)/shard_map/psum | solution.py:195
  376.6 2.5 copy-start.7
Sparse Core Ops, SparseCore 0:
  10.8 79.2 all-gather.7
  94.7 84.3 all-gather.9
  206.9 51.7 all-gather.11
  278.2 98.2 all-reduce.2
  380.4 195.3 all-reduce.4
